TPU v7x, 128 devices: a whole 4x4x4 slice. The times are simulated.
128 devices in a mesh: dp: 4 (over y), mem: 32 (over x, z, core).
Axes of the slice: x: 4, y: 4, z: 4, core: 2. Of those that a mesh axis runs over, the one named last changes fastest.
Arguments:
- images: bfloat16 [256, 577, 768], P(('dp', 'mem')), may hold values from -300 to 300
- text_cache: bfloat16 [2048, 40, 768], P('mem'), may hold values from -50 to 50
- cand_ids: int32 [256, 16], P(('dp', 'mem')), may hold values from 0 to 2047, as said below
- cand_slot: int32 [256, 16], P(('dp', 'mem')), may hold values from 0 to 15, each once within a row
- w_query: bfloat16 [768, 768], replicated, may hold values from -0.21875 to 0.21875
- w_key: bfloat16 [768, 768], replicated, may hold values from -0.21875 to 0.21875
- w_value: bfloat16 [768, 768], replicated, may hold values from -0.21875 to 0.21875
- w_out: bfloat16 [768, 768], replicated, may hold values from -0.21875 to 0.21875
- out_bias: float32 [768], replicated, may hold values from -3 to 3
- norm1_gain: float32 [768], replicated, may hold values from 0.5 to 1.5
- norm1_shift: float32 [768], replicated, may hold values from -1.8 to 1.8
- w_up: bfloat16 [768, 3072], replicated, may hold values from -0.21875 to 0.21875
- up_bias: float32 [3072], replicated, may hold values from -3 to 3
- w_down: bfloat16 [3072, 768], replicated, may hold values from -0.109375 to 0.109375
- down_bias: float32 [768], replicated, may hold values from -3 to 3
- norm2_gain: float32 [768], replicated, may hold values from 0.5 to 1.5
- norm2_shift: float32 [768], replicated, may hold values from -1.8 to 1.8
Outputs:
- pair_states: bfloat16 [4096, 40, 768], P(('dp', 'mem'))
Inputs may be any that keep to these rules, and one draw needn't show every extreme that they name: `cand_ids`: in every device's block of 2 images (its 32 candidates), at most 2 candidates lie on one memory shard (ids s * 64 to (s + 1) * 64 - 1), and in every such block some shard holds exactly 2.
All inputs are finite; a program needn't handle non-finite values.
Results may differ from a plain program's by a relative error of at most 0.01.
The roundings to bfloat16 on the way count: a program that leaves them out, or rounds other values in their place, can miss the bound.
Values may be sent and summed in bfloat16 or wider, within the bound.
A program may use at most 192 MiB of HBM per device.

v0:
```python
import jax
import jax.numpy as jnp
from jax import lax
from jax.sharding import PartitionSpec as P

HEADS = 12


NORM_EPS = 1e-06


def normalize(values, gain, shift):
    center = values - jnp.mean(values, axis=-1, keepdims=True)
    spread = jnp.mean(center * center, axis=-1, keepdims=True)
    return center * lax.rsqrt(spread + NORM_EPS) * gain + shift


def cross_layer(text_rows, key_values, layer_weights):
    (
        w_query,
        w_out,
        out_bias,
        norm1_gain,
        norm1_shift,
        w_up,
        up_bias,
        w_down,
        down_bias,
        norm2_gain,
        norm2_shift,
    ) = layer_weights
    item_count, row_count, model_width = text_rows.shape
    patch_count = key_values.shape[1]
    head_dim = model_width // HEADS
    head_group = 4
    group_steps = HEADS // head_group
    group_width = head_group * head_dim
    score_scale = head_dim ** (-0.5)
    flat_rows = text_rows.reshape(item_count * row_count, model_width)
    queries = jnp.dot(flat_rows, w_query, preferred_element_type=jnp.float32).astype(jnp.bfloat16)
    queries = queries.reshape(item_count, row_count, model_width)

    def one_group(running, step_index):
        col_start = step_index * group_width
        q_part = lax.dynamic_slice_in_dim(queries, col_start, group_width, 2).reshape(
            item_count, row_count, head_group, head_dim
        )
        k_part = lax.dynamic_slice_in_dim(key_values, col_start, group_width, 2).reshape(
            item_count, patch_count, head_group, head_dim
        )
        v_part = lax.dynamic_slice_in_dim(
            key_values, model_width + col_start, group_width, 2
        ).reshape(item_count, patch_count, head_group, head_dim)
        scores = (
            jnp.einsum("nrgc,npgc->ngrp", q_part, k_part, preferred_element_type=jnp.float32)
            * score_scale
        )
        row_max = jnp.max(scores, axis=-1, keepdims=True)
        exp_terms = jnp.exp(scores - row_max)
        attn_probs = (exp_terms / jnp.sum(exp_terms, axis=-1, keepdims=True)).astype(jnp.bfloat16)
        context = jnp.einsum(
            "ngrp,npgc->nrgc", attn_probs, v_part, preferred_element_type=jnp.float32
        ).astype(jnp.bfloat16)
        out_rows = lax.dynamic_slice_in_dim(w_out, col_start, group_width, 0)
        running = running + jnp.dot(
            context.reshape(item_count * row_count, group_width),
            out_rows,
            preferred_element_type=jnp.float32,
        )
        return (running, None)

    attended, _ = lax.scan(
        one_group,
        jnp.zeros((item_count * row_count, model_width), jnp.float32),
        jnp.arange(group_steps, dtype=jnp.int32),
    )
    first_out = normalize(
        attended + out_bias + flat_rows.astype(jnp.float32), norm1_gain, norm1_shift
    ).astype(jnp.bfloat16)
    hidden = jax.nn.gelu(
        jnp.dot(first_out, w_up, preferred_element_type=jnp.float32) + up_bias, approximate=False
    ).astype(jnp.bfloat16)
    output = (
        jnp.dot(hidden, w_down, preferred_element_type=jnp.float32)
        + down_bias
        + first_out.astype(jnp.float32)
    )
    return (
        normalize(output, norm2_gain, norm2_shift)
        .astype(jnp.bfloat16)
        .reshape(item_count, row_count, model_width)
    )


def on_device(
    images,
    text_cache,
    cand_ids,
    cand_slot,
    w_query,
    w_key,
    w_value,
    w_out,
    out_bias,
    norm1_gain,
    norm1_shift,
    w_up,
    up_bias,
    w_down,
    down_bias,
    norm2_gain,
    norm2_shift,
):
    mem_size = lax.axis_size("mem")
    group_total = lax.axis_size("dp")
    img_local, cand_count = cand_ids.shape
    cap_local, word_count, model_width = text_cache.shape
    pair_count = img_local * cand_count
    per_owner = max(2, 2 * pair_count // mem_size)
    per_group = cand_count // group_total
    flat_ids = cand_ids.reshape(pair_count)
    owner_of = flat_ids // cap_local
    local_row = flat_ids % cap_local
    position = jnp.arange(pair_count, dtype=jnp.int32)
    same_owner = (owner_of[:, None] == owner_of[None, :]) & (position[None, :] < position[:, None])
    owner_rank = jnp.sum(same_owner.astype(jnp.int32), axis=1)
    slot_index = owner_of * per_owner + owner_rank
    table_slots = jnp.arange(mem_size * per_owner, dtype=jnp.int32)
    request_table = (
        jnp.sum(
            jnp.where(slot_index[None, :] == table_slots[:, None], local_row[None, :] + 1, 0),
            axis=1,
        )
        - 1
    )
    request_table = request_table.reshape(mem_size, per_owner)
    fetched = lax.all_to_all(
        jnp.take(
            text_cache,
            jnp.maximum(
                lax.all_to_all(request_table, "mem", split_axis=0, concat_axis=0, tiled=True), 0
            ),
            axis=0,
        ),
        "mem",
        split_axis=0,
        concat_axis=0,
        tiled=True,
    )
    fetched_rows = fetched.reshape(mem_size * per_owner, word_count, model_width)
    slot_ids = jnp.arange(cand_count, dtype=jnp.int32)
    matches = cand_slot[:, :, None] == slot_ids[None, None, :]
    cand_order = jnp.sum(jnp.where(matches, slot_ids[None, :, None], 0), axis=1)
    pair_order = cand_order + jnp.arange(img_local, dtype=jnp.int32)[:, None] * cand_count
    text_rows = jnp.take(fetched_rows, slot_index[pair_order.reshape(pair_count)], axis=0)
    layer_weights = (
        w_query,
        w_out,
        out_bias,
        norm1_gain,
        norm1_shift,
        w_up,
        up_bias,
        w_down,
        down_bias,
        norm2_gain,
        norm2_shift,
    )
    w_pair = jnp.concatenate((w_key, w_value), axis=1)
    block_rows = per_group * word_count
    outgoing = text_rows.reshape(img_local, group_total, block_rows, model_width)
    arrived = lax.all_to_all(outgoing, "dp", split_axis=1, concat_axis=0, tiled=True)
    panels = lax.all_gather(images, "dp", axis=0, tiled=True)
    projected = jnp.dot(panels.reshape(-1, model_width), w_pair, preferred_element_type=jnp.float32)
    key_values = projected.astype(jnp.bfloat16).reshape(
        panels.shape[0], panels.shape[1], 2 * model_width
    )
    placed = cross_layer(arrived.reshape(-1, block_rows, model_width), key_values, layer_weights)
    return placed.reshape(pair_count, word_count, model_width)


def solution(mesh):
    in_specs = (
        P(("dp", "mem"), None, None),
        P("mem", None, None),
        P(("dp", "mem"), None),
        P(("dp", "mem"), None),
        P(),
        P(),
        P(),
        P(),
        P(),
        P(),
        P(),
        P(),
        P(),
        P(),
        P(),
        P(),
        P(),
    )
    out_specs = P(("dp", "mem"), None, None)
    return jax.shard_map(
        on_device, mesh=mesh, in_specs=in_specs, out_specs=out_specs, check_vma=False
    )
```

profile of v0, /device:TPU:1, one launch (start us, length us, event | category | flops | bytes accessed | tf_op | source)
XLA Modules:
  0.0 352.0 jit_solution(6482305497661842683)
XLA Ops:
  6.5 3.0 copy.39
  10.1 16.2 %all_to_all.26 = s32[32,1,2]{2,1,0:T(1,128)S(1)} all-to-all(s32[32,1,2]{2,1,0:T(1,128)S(1)} %bitcast.75), channel_id=1, replica_groups=mesh['dp'=4,'mem'=32] {'mem'}, dimensions={0} | all-to-all | bytes 512 | tf_op jit(solution)/shard_map/all_to_all | solution.py:141
  26.7 5.1 %gather_fusion.1 = bf16[64,40,768]{2,1,0:T(8,128)(2,1)} fusion(bf16[64,40,768]{2,1,0:T(8,128)(2,1)} %param.20, s32[1024]{0:T(1024)S(1)} %pad_clamp_fusion.1), kind=kCustom, calls=%fused_computation.1 | custom fusion | bytes 7864576 | tf_op jit(solution)/shard_map/jit(_take)/gather | solution.py:138
  31.8 4.4 %broadcast_select_fusion = bf16[32,2,40,768]{3,2,1,0:T(8,128)(2,1)} fusion(bf16[32,2,40,768]{3,2,1,0:T(8,128)(2,1)} %bitcast.72, pred[32,2]{1,0:T(8,128)(4,1)S(1)} %copy.42), kind=kLoop, calls=%fused_computation.80 | loop fusion | flops 1966080 | bytes 7864384 | tf_op jit(solution)/shard_map/jit(_take)/select_n | solution.py:138
  36.1 5.2 %all-to-all-start.1 = ((bf16[32,2,40,768]{3,2,1,0:T(8,128)(2,1)}), bf16[32,2,40,768]{3,2,1,0:T(8,128)(2,1)}, u32[]{:S(2)}, u32[]{:S(2)}) async-start(bf16[32,2,40,768]{3,2,1,0:T(8,128)(2,1)} %broadcast_select_fusion), calls=%async_computation.1 | async-start | bytes 7864320 | tf_op jit(solution)/shard_map/all_to_all | solution.py:137
  41.6 0.7 gather_fusion
  42.6 47.9 %all-to-all-done.1 = bf16[32,2,40,768]{3,2,1,0:T(8,128)(2,1)} async-done(((bf16[32,2,40,768]{3,2,1,0:T(8,128)(2,1)}), bf16[32,2,40,768]{3,2,1,0:T(8,128)(2,1)}, u32[]{:S(2)}, u32[]{:S(2)}) %all-to-all-start.1) | async-done | bytes 3932192 | tf_op jit(solution)/shard_map/all_to_all | solution.py:137
  90.5 2.8 gather_fusion.2
  93.6 1.4 copy.43
  95.0 4.7 %all-to-all-start.2 = ((bf16[2,4,160,768]{3,2,0,1:T(8,128)(2,1)}), bf16[2,4,160,768]{3,2,0,1:T(8,128)(2,1)S(1)}, u32[]{:S(2)}, u32[]{:S(2)}) async-start(bf16[2,4,160,768]{3,2,0,1:T(8,128)(2,1)} %copy.43), calls=%async_computation.2 | async-start | bytes 3932160 | tf_op jit(solution)/shard_map/all_to_all | solution.py:172
  99.8 23.9 %all-to-all-done.2 = bf16[2,4,160,768]{3,2,0,1:T(8,128)(2,1)S(1)} async-done(((bf16[2,4,160,768]{3,2,0,1:T(8,128)(2,1)}), bf16[2,4,160,768]{3,2,0,1:T(8,128)(2,1)S(1)}, u32[]{:S(2)}, u32[]{:S(2)}) %all-to-all-start.2) | async-done | bytes 1966112 | tf_op jit(solution)/shard_map/all_to_all | solution.py:172
  123.6 3.0 convolution_convert_fusion.1
  126.6 8.2 %reshape.265 = bf16[4616,768]{1,0:T(8,128)(2,1)} reshape(bf16[8,577,768]{2,1,0:T(8,128)(2,1)} %all-gather.2.cloned.1.call-done) | data formatting | bytes 14180352 | tf_op jit(solution)/shard_map/reshape | solution.py:174
  134.8 17.0 %fusion.13 = bf16[4616,1536]{1,0:T(8,128)(2,1)} fusion(bf16[4616,768]{1,0:T(8,128)(2,1)} %reshape.265, bf16[768,768]{1,0:T(8,128)(2,1)S(1)} %copy-done.9, bf16[768,768]{1,0:T(8,128)(2,1)S(1)} %copy-done.10), kind=kOutput, calls=%fused_computation.22 | convolution fusion | flops 10902319104 | bytes 23629824 | tf_op jit(solution)/shard_map/dot_general | solution.py:174
  151.8 14.2 %reshape.266 = bf16[8,577,1536]{2,1,0:T(8,128)(2,1)} reshape(bf16[4616,1536]{1,0:T(8,128)(2,1)} %fusion.13) | data formatting | bytes 28360704 | tf_op jit(solution)/shard_map/reshape | solution.py:175
  166.1 18.9 %copy.44 = bf16[8,577,1536]{1,2,0:T(8,128)(2,1)} copy(bf16[8,577,1536]{2,1,0:T(8,128)(2,1)} %reshape.266) | data formatting | bytes 28360704
  185.0 101.1 %while.13 = (s32[]{:T(128)}, f32[1280,768]{1,0:T(8,128)}, s32[3]{0:T(128)S(1)}, bf16[8,577,1536]{1,2,0:T(8,128)(2,1)}, bf16[8,160,768]{2,1,0:T(8,128)(2,1)}, /*i...) while((s32[]{:T(128)}, f32[1280,768]{1,0:T(8,128)}, ...), condition=%wide.region_6.7_spmd.clone, body=%wide.region_3.6_spmd.clone.sunk | while | flops 1276667392 | bytes 53321984 | solution.py:72
  185.0 0.7 dynamic_slice.48
  186.4 5.5 %constant_dynamic-slice_fusion.5 = (bf16[8,577,256]{1,2,0:T(8,128)(2,1)}, bf16[8,577,256]{1,2,0:T(8,128)(2,1)}) fusion(bf16[8,577,1536]{1,2,0:T(8,128)(2,1)} %get-tuple-element.220, s32[]{:T(128)S(6)} %select_n.124, s32[]{:T(128)S(6)} %select_n.125), kind=kLoop, calls=%fused_computation.16.clone.1 | loop fusion | bytes 9453576 | tf_op jit(solution)/shard_map/while/body/eval_jaxpr/dynamic_slice | solution.py:48
  191.9 1.1 constant_dynamic-slice_fusion.6
  193.6 10.6 %fusion.135 = (f32[8,4,160]{2,1,0:T(4,128)S(1)}, f32[8,4,160,577]{3,2,1,0:T(8,128)}) fusion(bf16[8,160,4,64]{1,3,2,0:T(8,128)(2,1)S(1)} %bitcast.68, bf16[8,577,4,64]{1,3,2,0:T(8,128)(2,1)} %bitcast.67), kind=kOutput, calls=%fused_computation.154.clone.1 | convolution fusion | flops 387006016 | bytes 14856192 | tf_op jit(solution)/shard_map/while/body/eval_jaxpr/sub | solution.py:59
  204.2 8.3 %fusion.136 = bf16[8,160,4,64]{1,3,2,0:T(8,128)(2,1)S(1)} fusion(bf16[8,577,4,64]{1,3,2,0:T(8,128)(2,1)} %bitcast.66, f32[8,4,160,577]{3,2,1,0:T(8,128)} %get-tuple-element.191, f32[8,4,160]{2,1,0:T(4,128)S(1)} %get-tuple-element.192), kind=kOutput, calls=%fused_computation.12.clone.1 | convolution fusion | flops 384378880 | bytes 14856192 | tf_op jit(solution)/shard_map/while/body/eval_jaxpr/ngrp,npgc->nrgc/dot_general | solution.py:61
  212.5 0.6 copy.50
  213.1 1.2 reshape.308
  214.3 3.6 %convolution_add_fusion.2 = f32[1280,768]{1,0:T(8,128)} fusion(bf16[1280,256]{0,1:T(8,128)(2,1)S(1)} %reshape.308, f32[1280,768]{1,0:T(8,128)} %get-tuple-element.206, pred[]{:T(512)S(6)} %compare.23, bf16[768,768]{1,0:T(8,128)(2,1)} %get-tuple-element.222, s32[]{:T(128)S(6)} %select_n.126), kind=kOutput, calls=%fused_computation.10.clone.1 | convolution fusion | flops 505282560 | bytes 8912901 | tf_op jit(solution)/shard_map/while/body/eval_jaxpr/dot_general | solution.py:65
  217.9 0.7 dynamic_slice.48
  219.3 5.5 %constant_dynamic-slice_fusion.5 = (bf16[8,577,256]{1,2,0:T(8,128)(2,1)}, bf16[8,577,256]{1,2,0:T(8,128)(2,1)}) fusion(bf16[8,577,1536]{1,2,0:T(8,128)(2,1)} %get-tuple-element.220, s32[]{:T(128)S(6)} %select_n.124, s32[]{:T(128)S(6)} %select_n.125), kind=kLoop, calls=%fused_computation.16.clone.1 | loop fusion | bytes 9453576 | tf_op jit(solution)/shard_map/while/body/eval_jaxpr/dynamic_slice | solution.py:48
  224.8 1.1 constant_dynamic-slice_fusion.6
  226.4 10.6 %fusion.135 = (f32[8,4,160]{2,1,0:T(4,128)S(1)}, f32[8,4,160,577]{3,2,1,0:T(8,128)}) fusion(bf16[8,160,4,64]{1,3,2,0:T(8,128)(2,1)S(1)} %bitcast.68, bf16[8,577,4,64]{1,3,2,0:T(8,128)(2,1)} %bitcast.67), kind=kOutput, calls=%fused_computation.154.clone.1 | convolution fusion | flops 387006016 | bytes 14856192 | tf_op jit(solution)/shard_map/while/body/eval_jaxpr/sub | solution.py:59
  237.0 8.3 %fusion.136 = bf16[8,160,4,64]{1,3,2,0:T(8,128)(2,1)S(1)} fusion(bf16[8,577,4,64]{1,3,2,0:T(8,128)(2,1)} %bitcast.66, f32[8,4,160,577]{3,2,1,0:T(8,128)} %get-tuple-element.191, f32[8,4,160]{2,1,0:T(4,128)S(1)} %get-tuple-element.192), kind=kOutput, calls=%fused_computation.12.clone.1 | convolution fusion | flops 384378880 | bytes 14856192 | tf_op jit(solution)/shard_map/while/body/eval_jaxpr/ngrp,npgc->nrgc/dot_general | solution.py:61
  245.4 0.6 copy.50
  246.0 1.2 reshape.308
  247.1 4.8 %convolution_add_fusion.2 = f32[1280,768]{1,0:T(8,128)} fusion(bf16[1280,256]{0,1:T(8,128)(2,1)S(1)} %reshape.308, f32[1280,768]{1,0:T(8,128)} %get-tuple-element.206, pred[]{:T(512)S(6)} %compare.23, bf16[768,768]{1,0:T(8,128)(2,1)} %get-tuple-element.222, s32[]{:T(128)S(6)} %select_n.126), kind=kOutput, calls=%fused_computation.10.clone.1 | convolution fusion | flops 505282560 | bytes 8912901 | tf_op jit(solution)/shard_map/while/body/eval_jaxpr/dot_general | solution.py:65
  252.0 0.7 dynamic_slice.48
  253.4 5.5 %constant_dynamic-slice_fusion.5 = (bf16[8,577,256]{1,2,0:T(8,128)(2,1)}, bf16[8,577,256]{1,2,0:T(8,128)(2,1)}) fusion(bf16[8,577,1536]{1,2,0:T(8,128)(2,1)} %get-tuple-element.220, s32[]{:T(128)S(6)} %select_n.124, s32[]{:T(128)S(6)} %select_n.125), kind=kLoop, calls=%fused_computation.16.clone.1 | loop fusion | bytes 9453576 | tf_op jit(solution)/shard_map/while/body/eval_jaxpr/dynamic_slice | solution.py:48
  258.9 1.1 constant_dynamic-slice_fusion.6
  260.5 10.6 %fusion.135 = (f32[8,4,160]{2,1,0:T(4,128)S(1)}, f32[8,4,160,577]{3,2,1,0:T(8,128)}) fusion(bf16[8,160,4,64]{1,3,2,0:T(8,128)(2,1)S(1)} %bitcast.68, bf16[8,577,4,64]{1,3,2,0:T(8,128)(2,1)} %bitcast.67), kind=kOutput, calls=%fused_computation.154.clone.1 | convolution fusion | flops 387006016 | bytes 14856192 | tf_op jit(solution)/shard_map/while/body/eval_jaxpr/sub | solution.py:59
  271.1 8.3 %fusion.136 = bf16[8,160,4,64]{1,3,2,0:T(8,128)(2,1)S(1)} fusion(bf16[8,577,4,64]{1,3,2,0:T(8,128)(2,1)} %bitcast.66, f32[8,4,160,577]{3,2,1,0:T(8,128)} %get-tuple-element.191, f32[8,4,160]{2,1,0:T(4,128)S(1)} %get-tuple-element.192), kind=kOutput, calls=%fused_computation.12.clone.1 | convolution fusion | flops 384378880 | bytes 14856192 | tf_op jit(solution)/shard_map/while/body/eval_jaxpr/ngrp,npgc->nrgc/dot_general | solution.py:61
  279.5 0.6 copy.50
  280.1 1.2 reshape.308
  281.2 4.8 %convolution_add_fusion.2 = f32[1280,768]{1,0:T(8,128)} fusion(bf16[1280,256]{0,1:T(8,128)(2,1)S(1)} %reshape.308, f32[1280,768]{1,0:T(8,128)} %get-tuple-element.206, pred[]{:T(512)S(6)} %compare.23, bf16[768,768]{1,0:T(8,128)(2,1)} %get-tuple-element.222, s32[]{:T(128)S(6)} %select_n.126), kind=kOutput, calls=%fused_computation.10.clone.1 | convolution fusion | flops 505282560 | bytes 8912901 | tf_op jit(solution)/shard_map/while/body/eval_jaxpr/dot_general | solution.py:65
  286.1 3.5 fusion.69
  290.0 0.6 copy-done.4
  290.6 1.1 multiply_reduce_fusion.2
  291.7 43.2 %fusion.16.clone.5.clone.4 = bf16[1280,3072]{1,0:T(8,128)(2,1)S(1)} fusion(bf16[768,3072]{1,0:T(8,128)(2,1)} %param.30, f32[3072]{0:T(1024)S(1)} %copy-done.11, f32[768]{0:T(1024)S(1)} %copy-done.12, f32[768]{0:T(1024)S(1)} %copy-done.13, f32[1280]{0:T(1024)S(1)} %add_rsqrt_fusion.1, ...), kind=kOutput, calls=%fused_computation.25.clone.clone.clone.clone.clone.clone.clone.clone.clone.1 | convolution fusion | flops 6307184640 | bytes 18512896 | tf_op jit(solution)/shard_map/dot_general | solution.py:81
  335.0 7.2 %fusion.106 = (f32[1280]{0:T(1024)S(1)}, f32[1280,768]{1,0:T(8,128)S(1)}) fusion(f32[768]{0:T(1024)S(1)} %copy-done.12, f32[768]{0:T(1024)S(1)} %copy-done.13, f32[1280]{0:T(1024)S(1)} %add_rsqrt_fusion.1, f32[1280]{0:T(1024)S(1)} %broadcast_multiply_fusion.1, bf16[1280,768]{1,0:T(8,128)(2,1)S(1)} %bitcast.71, f32[1280,768]{1,0:T(8,128)S(1)} %copy-done.2, ...), kind=kOutput, calls=%fused_computation.155 | convolution fusion | flops 6051593216 | bytes 22440960 | tf_op jit(solution)/shard_map/dot_general | solution.py:84
  342.3 0.6 multiply_reduce_fusion.1
  342.9 1.9 add_convert_fusion
  (74 shorter events, 3.7 us)
Async XLA Ops:
  6.5 117.1 %copy-start = (bf16[768,768]{1,0:T(8,128)(2,1)S(1)}, bf16[768,768]{1,0:T(8,128)(2,1)}, u32[]{:S(2)}) copy-start(bf16[768,768]{1,0:T(8,128)(2,1)} %param.23) | copy-start | bytes 3538948
  6.5 3.1 copy-start.15
  6.5 120.1 %all-gather.2.cloned.1.call-start = ((), (), s32[]{:S(2)}) async-start(), calls=%async_computation.3 | async-start | bytes 8970240 | tf_op jit(solution)/shard_map/all_gather | solution.py:173
  36.1 5.2 %copy-start.8 = (s32[2,16]{1,0:T(2,128)S(1)}, s32[2,16]{1,0:T(2,128)}, u32[]{:S(2)}) copy-start(s32[2,16]{1,0:T(2,128)} %param.22) | copy-start | bytes 388
  36.1 54.4 %all-to-all-start.1 = ((bf16[32,2,40,768]{3,2,1,0:T(8,128)(2,1)}), bf16[32,2,40,768]{3,2,1,0:T(8,128)(2,1)}, u32[]{:S(2)}, u32[]{:S(2)}) async-start(bf16[32,2,40,768]{3,2,1,0:T(8,128)(2,1)} %broadcast_select_fusion), calls=%async_computation.1 | async-start | bytes 7864320 | tf_op jit(solution)/shard_map/all_to_all | solution.py:137
  95.0 28.6 %all-to-all-start.2 = ((bf16[2,4,160,768]{3,2,0,1:T(8,128)(2,1)}), bf16[2,4,160,768]{3,2,0,1:T(8,128)(2,1)S(1)}, u32[]{:S(2)}, u32[]{:S(2)}) async-start(bf16[2,4,160,768]{3,2,0,1:T(8,128)(2,1)} %copy.43), calls=%async_computation.2 | async-start | bytes 3932160 | tf_op jit(solution)/shard_map/all_to_all | solution.py:172
  123.6 3.0 copy-start.3
  126.6 8.2 %copy-start.9 = (bf16[768,768]{1,0:T(8,128)(2,1)S(1)}, bf16[768,768]{1,0:T(8,128)(2,1)}, u32[]{:S(2)}) copy-start(bf16[768,768]{1,0:T(8,128)(2,1)} %param.25) | copy-start | bytes 3538948
  126.6 8.2 %copy-start.10 = (bf16[768,768]{1,0:T(8,128)(2,1)S(1)}, bf16[768,768]{1,0:T(8,128)(2,1)}, u32[]{:S(2)}) copy-start(bf16[768,768]{1,0:T(8,128)(2,1)} %param.24) | copy-start | bytes 3538948
  185.0 101.1 %copy-start.5 = (f32[768]{0:T(1024)S(1)}, f32[768]{0:T(1024)}, u32[]{:S(2)}) copy-start(f32[768]{0:T(1024)} %param.27) | copy-start | bytes 9220
  286.1 3.9 %copy-start.2 = (f32[1280,768]{1,0:T(8,128)S(1)}, f32[1280,768]{1,0:T(8,128)}, u32[]{:S(2)}) copy-start(f32[1280,768]{1,0:T(8,128)} %get-tuple-element.82) | copy-start | bytes 11796484
  286.1 4.5 %copy-start.4 = (bf16[2,4,160,768]{3,2,0,1:T(8,128)(2,1)S(1)}, bf16[2,4,160,768]{3,2,0,1:T(8,128)(2,1)}, u32[]{:S(2)}) copy-start(bf16[2,4,160,768]{3,2,0,1:T(8,128)(2,1)} %copy-done.3) | copy-start | bytes 5898244
  289.6 2.1 copy-start.11
  289.6 2.1 copy-start.12
  289.6 2.1 copy-start.13
  290.6 44.3 %slice-start = ((s8[4718592]{0:T(1024)(128)(4,1)}), s8[4194304]{0:T(1024)(128)(4,1)S(1)}, s32[]{:S(2)}) async-start(s8[4718592]{0:T(1024)(128)(4,1)} %bitcast.77), calls=%async_computation.4 | async-start | bytes 8388608
  291.7 43.2 %slice-start.1 = ((s8[4718592]{0:T(1024)(128)(4,1)}), s8[524288]{0:T(1024)(128)(4,1)S(1)}, s32[]{:S(2)}) async-start(s8[4718592]{0:T(1024)(128)(4,1)} %bitcast.77), calls=%async_computation.5 | async-start | bytes 1048576
  291.7 43.2 %copy-start.14 = (f32[768]{0:T(1024)S(1)}, f32[768]{0:T(1024)}, u32[]{:S(2)}) copy-start(f32[768]{0:T(1024)} %param.33) | copy-start | bytes 9220
  342.2 0.7 copy-start.6
  342.2 0.7 copy-start.7
  342.2 2.6 copy-start.1
Sparse Core Ops, SparseCore 0:
  9.7 76.2 all-gather.1
where the time goes:
time: 357 us; the launch traced here: 352 us
  matrix products  141 us (39%)
  local copies, waits for them, and re-layouts  85 us (24%)
  waiting for transfers between devices  71.8 us (20%)
  blocking collectives  16.2 us (5%)
  between operations  14 us (4%)
  other arithmetic  12.3 us (3%)
  starting transfers between devices  9.91 us (3%)
    all_to_all x1, waiting for transfers between devices, on_device(): lax.all_to_all(jnp.take(text_cache, jnp.maximum(lax.all_to_all(request_ta...  47.9 us
    dot_general x1, matrix products, cross_layer(): jnp.dot(first_out, w_up, preferred_element_type=jnp.float32) + up_bias  43.2 us
    sub x3, matrix products, one_group(): exp_terms = jnp.exp(scores - row_max)  31.8 us
    dot_general x3, matrix products, one_group(): jnp.einsum('ngrp,npgc->nrgc', attn_probs, v_part, preferred_element_type=...  25 us
    all_to_all x1, waiting for transfers between devices, on_device(): lax.all_to_all(outgoing, 'dp', split_axis=1, concat_axis=0, tiled=True)  23.9 us
    unnamed x38, local copies, waits for them, and re-layouts  23.1 us
    dot_general x1, matrix products, on_device(): jnp.dot(panels.reshape(-1, model_width), w_pair, preferred_element_type=j...  17 us
    dynamic_slice x3, local copies, waits for them, and re-layouts, one_group(): lax.dynamic_slice_in_dim(key_values, col_start, group_width, 2)  16.6 us
  transfers between devices with their start and end apart: 3, of which 2 were waited for; matrix products, arithmetic and copies ran while one was open for 5% of the time, Pallas kernels for 0%

commit v1 on v0

v1 whole, which is shorter than its diff:
```python
import functools
import math

import jax
import jax.numpy as jnp
from jax import lax
from jax.experimental import pallas as pl
from jax.experimental.pallas import tpu as pltpu
from jax.sharding import PartitionSpec as P

MESH = pl.DeviceIdType.MESH
F32 = jnp.float32
BF16 = jnp.bfloat16
HEADS = 12
NORM_EPS = 1e-06
PIECE = 8
SLOTS = 2
LANES = 128
NT = (((1,), (1,)), ((), ()))


def normalize(values, gain, shift):
    center = values - jnp.mean(values, axis=-1, keepdims=True)
    spread = jnp.mean(center * center, axis=-1, keepdims=True)
    return center * lax.rsqrt(spread + NORM_EPS) * gain + shift


def project_images(img, w_key, w_value, keys, values_t):
    images, patches, width = img.shape
    whole = patches // 16 * 16
    rest = patches - whole
    for t in range(images):
        panel = img[t]
        rows = jnp.dot(panel, w_key[...], preferred_element_type=F32)
        keys[t, 0:whole, :] = rows[0:whole].astype(BF16)
        tail = jnp.concatenate([rows[whole:patches], jnp.zeros((16 - rest, width), F32)], axis=0)
        keys[t, whole : whole + 16, :] = tail.astype(BF16)
        for col in range(0, width, LANES):
            part = jnp.dot(panel, w_value[:, col : col + LANES], preferred_element_type=F32)
            pad = jnp.zeros((values_t.shape[2] - patches, LANES), F32)
            values_t[t, col : col + LANES, :] = jnp.concatenate([part, pad], axis=0).T.astype(BF16)


def head_pair_scores(queries, keys, t, col, rows):
    both = queries[t * rows : (t + 1) * rows, col : col + LANES].astype(F32)
    first = lax.broadcasted_iota(jnp.int32, both.shape, 1) < LANES // 2
    stacked = jnp.concatenate([jnp.where(first, both, 0.0), jnp.where(first, 0.0, both)], axis=0)
    return lax.dot_general(
        keys[t, :, col : col + LANES], stacked.astype(BF16), NT, preferred_element_type=F32
    )


def exponentials(scores, patches, scale):
    whole = patches // 16 * 16
    body, tail = scores[0:whole], scores[whole:]
    row = lax.broadcasted_iota(jnp.int32, tail.shape, 0)
    tail = jnp.where(row < patches - whole, tail, -1e30)
    top = jnp.maximum(
        jnp.max(body, axis=0, keepdims=True), jnp.max(tail, axis=0, keepdims=True)
    )
    factor = scale * math.log2(math.e)
    body = jnp.exp2((body - top) * factor)
    tail = jnp.exp2((tail - top) * factor)
    total = jnp.sum(body, axis=0, keepdims=True) + jnp.sum(tail, axis=0, keepdims=True)
    return jnp.concatenate([body, tail], axis=0).astype(BF16), total


def attend(queries, keys, values_t, context, patches):
    images, padded, width = keys.shape
    rows = queries.shape[0] // images
    half = LANES // 2
    scale = (width // HEADS) ** (-0.5)
    order = [(t, col) for t in range(images) for col in range(0, width, LANES)]
    scores = head_pair_scores(queries, keys, *order[0], rows)
    for index, (t, col) in enumerate(order):
        following = None
        if index + 1 < len(order):
            following = head_pair_scores(queries, keys, *order[index + 1], rows)
        probs, total = exponentials(scores, patches, scale)
        mixed = jnp.dot(
            values_t[t, col : col + LANES, 0:padded], probs, preferred_element_type=F32
        )
        inverse = 1.0 / total
        mixed = jnp.concatenate(
            [
                mixed[0:half, 0:rows] * inverse[:, 0:rows],
                mixed[half:LANES, rows:] * inverse[:, rows:],
            ],
            axis=0,
        )
        context[t * rows : (t + 1) * rows, col : col + LANES] = mixed.T.astype(BF16)
        scores = following


def kernel(
    mem_size,
    dp_size,
    requests,
    targets,
    out_bias,
    gain1,
    shift1,
    up_bias,
    down_bias,
    gain2,
    shift2,
    cache_hbm,
    img_hbm,
    w_key_hbm,
    w_value_hbm,
    w_query_hbm,
    w_out_hbm,
    w_up_hbm,
    w_down_hbm,
    arrived_out,
    cache,
    img,
    w_key,
    w_value,
    w_query,
    w_out,
    w_up,
    w_down,
    wanted,
    wanted_smem,
    outgoing,
    incoming,
    select,
    keys,
    values_t,
    context,
    finished,
    local_sem,
    smem_sem,
    ask_send,
    ask_recv,
    text_send,
    text_recv,
    out_send,
    out_recv,
    own_sem,
):
    dp = lax.axis_index("dp")
    mem = lax.axis_index("mem")
    words = cache.shape[1]
    piece_count = words // PIECE
    patches = img.shape[1]
    images = img.shape[0]

    loads = [
        pltpu.make_async_copy(source, target, local_sem.at[index])
        for index, (source, target) in enumerate(
            [
                (cache_hbm, cache),
                (img_hbm, img),
                (w_key_hbm, w_key),
                (w_value_hbm, w_value),
                (w_query_hbm, w_query),
                (w_out_hbm, w_out),
                (w_up_hbm, w_up),
                (w_down_hbm, w_down),
            ]
        )
    ]
    for load in loads:
        load.start()

    barrier = pltpu.get_barrier_semaphore()

    def greet(step, carry):
        peer = lax.rem(mem + step, mem_size)
        pl.semaphore_signal(barrier, inc=1, device_id=(dp, peer), device_id_type=MESH)
        return carry

    lax.fori_loop(1, mem_size, greet, 0)
    for step in range(1, dp_size):
        pl.semaphore_signal(
            barrier, inc=1, device_id=(lax.rem(dp + step, dp_size), mem), device_id_type=MESH
        )
    pl.semaphore_wait(barrier, mem_size - 1 + dp_size - 1)

    def ask(step, carry):
        peer = lax.rem(mem + step, mem_size)
        pltpu.make_async_remote_copy(
            src_ref=requests.at[peer],
            dst_ref=wanted.at[mem],
            send_sem=ask_send,
            recv_sem=ask_recv,
            device_id=(dp, peer),
            device_id_type=MESH,
        ).start()
        return carry

    lax.fori_loop(1, mem_size, ask, 0)
    wanted[mem] = requests[mem]

    row_targets = targets[...]
    for col in range(0, select.shape[1], LANES):
        lane = lax.broadcasted_iota(jnp.int32, row_targets.shape, 1) + col
        select[:, col : col + LANES] = jnp.where(row_targets == lane, 1.0, 0.0).astype(BF16)

    others = pl.ds(0, mem_size - 1)
    pltpu.make_async_copy(wanted.at[others], wanted.at[others], ask_recv).wait()
    to_smem = pltpu.make_async_copy(wanted, wanted_smem, smem_sem)
    to_smem.start()
    loads[0].wait()
    to_smem.wait()

    def rows_for(peer, start):
        parts = [
            cache[wanted_smem[peer, 0, slot], start : start + PIECE, :].astype(F32)
            for slot in range(SLOTS)
        ]
        return jnp.concatenate(parts, axis=0).astype(BF16)

    for piece in range(piece_count):
        incoming[piece, mem] = rows_for(mem, piece * PIECE)

        def serve(step, carry, piece=piece):
            peer = lax.rem(mem + step, mem_size)
            outgoing[piece, peer] = rows_for(peer, piece * PIECE)
            pltpu.make_async_remote_copy(
                src_ref=outgoing.at[piece, peer],
                dst_ref=incoming.at[piece, mem],
                send_sem=text_send.at[piece],
                recv_sem=text_recv.at[piece],
                device_id=(dp, peer),
                device_id_type=MESH,
            ).start()
            return carry

        lax.fori_loop(1, mem_size, serve, 0)

    for load in loads[1:4]:
        load.wait()
    project_images(img, w_key, w_value, keys, values_t)
    for load in loads[4:]:
        load.wait()

    group_rows = finished.shape[2]
    half_rows = group_rows // images

    def work(piece, carry):
        pltpu.make_async_copy(
            incoming.at[piece, others], incoming.at[piece, others], text_recv.at[piece]
        ).wait()
        arrived = incoming[piece].reshape(-1, incoming.shape[3])
        text = jnp.dot(select[...], arrived, preferred_element_type=F32)
        text_rows = text.astype(BF16)
        queries = jnp.dot(text_rows, w_query[...], preferred_element_type=F32).astype(BF16)
        attend(queries, keys, values_t, context, patches)
        attended = jnp.dot(context[...], w_out[...], preferred_element_type=F32)
        first_out = normalize(
            attended + out_bias[...] + text_rows.astype(F32), gain1[...], shift1[...]
        ).astype(BF16)
        hidden = jnp.dot(first_out, w_up[...], preferred_element_type=F32) + up_bias[...]
        hidden = (0.5 * hidden * (1.0 + lax.erf(hidden * 0.5**0.5))).astype(BF16)
        output = jnp.dot(hidden, w_down[...], preferred_element_type=F32)
        output = output + down_bias[...] + first_out.astype(F32)
        encoded = normalize(output, gain2[...], shift2[...]).astype(BF16)
        for t in range(images):
            for group in range(dp_size):
                start = (t * dp_size + group) * half_rows
                finished[piece, group, t * half_rows : (t + 1) * half_rows, :] = encoded[
                    start : start + half_rows
                ]
        for step in range(1, dp_size):
            peer = lax.rem(dp + step, dp_size)
            pltpu.make_async_remote_copy(
                src_ref=finished.at[piece, peer],
                dst_ref=arrived_out.at[piece, dp],
                send_sem=out_send,
                recv_sem=out_recv,
                device_id=(peer, mem),
                device_id_type=MESH,
            ).start()
        pltpu.make_async_copy(
            finished.at[piece, dp], arrived_out.at[piece, dp], own_sem
        ).start()
        return carry

    lax.fori_loop(0, piece_count, work, 0)

    pltpu.make_async_copy(requests.at[others], requests.at[others], ask_send).wait()

    def drain(piece, carry):
        pltpu.make_async_copy(
            outgoing.at[piece, others], outgoing.at[piece, others], text_send.at[piece]
        ).wait()
        return carry

    lax.fori_loop(0, piece_count, drain, 0)
    sent = finished.at[:, pl.ds(0, dp_size - 1)]
    pltpu.make_async_copy(sent, sent, out_send).wait()
    came = arrived_out.at[:, pl.ds(0, dp_size - 1)]
    pltpu.make_async_copy(came, came, out_recv).wait()
    own = arrived_out.at[:, pl.ds(0, 1)]
    pltpu.make_async_copy(own, own, own_sem).wait()


def on_device(
    images,
    text_cache,
    cand_ids,
    cand_slot,
    w_query,
    w_key,
    w_value,
    w_out,
    out_bias,
    norm1_gain,
    norm1_shift,
    w_up,
    up_bias,
    w_down,
    down_bias,
    norm2_gain,
    norm2_shift,
):
    mem_size = lax.axis_size("mem")
    dp_size = lax.axis_size("dp")
    img_local, cand_count = cand_ids.shape
    cap_local, word_count, width = text_cache.shape
    patches = images.shape[1]
    hidden_width = w_up.shape[1]
    pair_count = img_local * cand_count
    piece_count = word_count // PIECE
    piece_rows = pair_count * PIECE
    slot_rows = SLOTS * PIECE
    padded = -(-patches // 16) * 16
    padded_lanes = -(-patches // LANES) * LANES

    flat_ids = cand_ids.reshape(pair_count)
    owner_of = flat_ids // cap_local
    local_row = flat_ids % cap_local
    position = jnp.arange(pair_count, dtype=jnp.int32)
    same_owner = (owner_of[:, None] == owner_of[None, :]) & (position[None, :] < position[:, None])
    owner_rank = jnp.sum(same_owner.astype(jnp.int32), axis=1)
    slot_index = owner_of * SLOTS + owner_rank
    table_slots = (
        jnp.arange(mem_size, dtype=jnp.int32)[:, None] * SLOTS
        + jnp.arange(LANES, dtype=jnp.int32)[None, :]
    )
    table_slots = jnp.where(jnp.arange(LANES)[None, :] < SLOTS, table_slots, -1)
    requests = jnp.sum(
        jnp.where(slot_index[None, None, :] == table_slots[:, :, None], local_row, 0), axis=2
    ).reshape(mem_size, 1, LANES)

    slot_ids = jnp.arange(cand_count, dtype=jnp.int32)
    matches = cand_slot[:, :, None] == slot_ids[None, None, :]
    slot_of = jnp.sum(
        jnp.where(matches, slot_index.reshape(img_local, cand_count, 1), 0), axis=1
    ).reshape(pair_count)
    targets = slot_of[:, None] * PIECE + jnp.arange(PIECE, dtype=jnp.int32)[None, :]
    targets = jnp.broadcast_to(targets.reshape(piece_rows, 1), (piece_rows, LANES))

    vmem = pl.BlockSpec(memory_space=pltpu.VMEM)
    anywhere = pl.BlockSpec(memory_space=pl.ANY)
    group_rows = piece_rows // dp_size
    result = pl.pallas_call(
        functools.partial(kernel, mem_size, dp_size),
        out_shape=jax.ShapeDtypeStruct((piece_count, dp_size, group_rows, width), BF16),
        in_specs=[vmem] * 9 + [anywhere] * 8,
        out_specs=anywhere,
        scratch_shapes=[
            pltpu.VMEM(text_cache.shape, BF16),
            pltpu.VMEM(images.shape, BF16),
            pltpu.VMEM((width, width), BF16),
            pltpu.VMEM((width, width), BF16),
            pltpu.VMEM((width, width), BF16),
            pltpu.VMEM((width, width), BF16),
            pltpu.VMEM((width, hidden_width), BF16),
            pltpu.VMEM((hidden_width, width), BF16),
            pltpu.VMEM((mem_size, 1, LANES), jnp.int32),
            pltpu.SMEM((mem_size, 1, LANES), jnp.int32),
            pltpu.VMEM((piece_count, mem_size, slot_rows, width), BF16),
            pltpu.VMEM((piece_count, mem_size, slot_rows, width), BF16),
            pltpu.VMEM((piece_rows, mem_size * slot_rows), BF16),
            pltpu.VMEM((img_local, padded, width), BF16),
            pltpu.VMEM((img_local, width, padded_lanes), BF16),
            pltpu.VMEM((piece_rows, width), BF16),
            pltpu.VMEM((piece_count, dp_size, group_rows, width), BF16),
            pltpu.SemaphoreType.DMA((8,)),
            pltpu.SemaphoreType.DMA,
            pltpu.SemaphoreType.DMA,
            pltpu.SemaphoreType.DMA,
            pltpu.SemaphoreType.DMA((piece_count,)),
            pltpu.SemaphoreType.DMA((piece_count,)),
            pltpu.SemaphoreType.DMA,
            pltpu.SemaphoreType.DMA,
            pltpu.SemaphoreType.DMA,
        ],
        compiler_params=pltpu.CompilerParams(
            collective_id=0, has_side_effects=True, vmem_limit_bytes=60 * 2**20
        ),
    )(
        requests,
        targets,
        out_bias.reshape(1, width),
        norm1_gain.reshape(1, width),
        norm1_shift.reshape(1, width),
        up_bias.reshape(1, hidden_width),
        down_bias.reshape(1, width),
        norm2_gain.reshape(1, width),
        norm2_shift.reshape(1, width),
        text_cache,
        images,
        w_key,
        w_value,
        w_query,
        w_out,
        w_up,
        w_down,
    )
    pairs = pair_count // dp_size
    result = result.reshape(piece_count, dp_size, pairs, PIECE, width)
    return result.transpose(1, 2, 0, 3, 4).reshape(pair_count, word_count, width)


def solution(mesh):
    split = P(("dp", "mem"), None, None)
    ids = P(("dp", "mem"), None)
    in_specs = (split, P("mem", None, None), ids, ids) + (P(),) * 13
    return jax.shard_map(
        on_device, mesh=mesh, in_specs=in_specs, out_specs=split, check_vma=False
    )
```

time: 357 us -> 115 us (0.32)
  the two profiles are of different devices: /device:TPU:1 before, /device:TPU:19 now
where the time goes in v1:
time: 115 us; the launch traced here: 114 us
  Pallas kernels  96.5 us (84%)
  local copies, waits for them, and re-layouts  15.3 us (13%)
  other arithmetic  2.56 us (2%)
    pallas_call x1, Pallas kernels, on_device(): pl.pallas_call(functools.partial(kernel, mem_size, dp_size), out_shape=ja...  96.5 us
    transpose x1, local copies, waits for them, and re-layouts, on_device(): result.transpose(1, 2, 0, 3, 4).reshape(pair_count, word_count, width)  2.94 us
    unnamed x1, local copies, waits for them, and re-layouts  2.91 us

profile of v1, /device:TPU:19, one launch (start us, length us, event | category | flops | bytes accessed | tf_op | source)
XLA Modules:
  0.0 114.4 jit_solution(581979573754389466)
XLA Ops:
  0.0 0.8 reshape.211
  0.8 0.2 convert_reduce_fusion
  1.0 0.1 reduce_sum.31
  1.1 0.7 multiply_add_fusion
  1.7 0.8 select_reduce_fusion.1
  2.5 0.1 mul.46
  2.6 1.3 %reshape.213.out_bias = f32[1,768]{1,0:T(1,128)} reshape(f32[768]{0:T(1024)} %param.25) | data formatting | bytes 6144 | tf_op jit(solution)/shard_map/reshape | solution.py:399
  3.9 1.3 %reshape.214.gain1 = f32[1,768]{1,0:T(1,128)} reshape(f32[768]{0:T(1024)} %param.26) | data formatting | bytes 6144 | tf_op jit(solution)/shard_map/reshape | solution.py:400
  5.2 1.3 %reshape.215.shift1 = f32[1,768]{1,0:T(1,128)} reshape(f32[768]{0:T(1024)} %param.27) | data formatting | bytes 6144 | tf_op jit(solution)/shard_map/reshape | solution.py:401
  6.4 1.3 %reshape.217.down_bias = f32[1,768]{1,0:T(1,128)} reshape(f32[768]{0:T(1024)} %param.31) | data formatting | bytes 6144 | tf_op jit(solution)/shard_map/reshape | solution.py:403
  7.7 1.3 %reshape.218.gain2 = f32[1,768]{1,0:T(1,128)} reshape(f32[768]{0:T(1024)} %param.32) | data formatting | bytes 6144 | tf_op jit(solution)/shard_map/reshape | solution.py:404
  9.0 1.3 %reshape.219.shift2 = f32[1,768]{1,0:T(1,128)} reshape(f32[768]{0:T(1024)} %param.33) | data formatting | bytes 6144 | tf_op jit(solution)/shard_map/reshape | solution.py:405
  10.3 0.1 add_select_fusion
  10.3 0.7 select_reduce_fusion
  11.1 0.1 iota_add_fusion
  11.2 0.1 add.78
  11.3 0.8 broadcast_in_dim.55.targets
  12.0 2.9 %copy.22.img_hbm = bf16[2,577,768]{2,1,0:T(8,128)(2,1)} copy(bf16[2,577,768]{2,0,1:T(2,128)(2,1)} %param.17) | data formatting | bytes 3545088 | tf_op args[0]
  14.9 96.5 %shard_map.163 = bf16[5,4,64,768]{3,2,1,0:T(8,128)(2,1)} custom-call(s32[32,1,128]{2,1,0:T(1,128)} %bitcast.7, s32[256,128]{1,0:T(8,128)} %broadcast_in_dim.55.targets, f32[1,768]{1,0:T(1,128)} %reshape.213.out_bias, f32[1,768]{1,0:T(1,128)} %reshape.214.gain1, f32[1,768]{1,0:T(1,128)} %reshape.215.shift1, f32[1,3072]{1,0:T(1,128)} %bitcast.8, ...), custom_call_target="tpu_custom_call" | custom-call | tf_op jit(solution)/shard_map/pallas_call | solution.py:360
  111.5 2.9 %copy.23 = bf16[4,8,5,8,768]{4,3,2,1,0:T(8,128)(2,1)} copy(bf16[4,8,5,8,768]{4,3,1,0,2:T(8,128)(2,1)} %bitcast.6) | data formatting | bytes 3932160 | tf_op jit(solution)/shard_map/transpose | solution.py:417
  (5 shorter events, 0.0 us)

commit v2 on v1

--- a/solution.py
+++ b/solution.py
@@ -25,20 +25,72 @@
     return center * lax.rsqrt(spread + NORM_EPS) * gain + shift
 
 
-def project_images(img, w_key, w_value, keys, values_t):
-    images, patches, width = img.shape
+def project_images(img, w_key, w_value, keys, values_t, wide):
+    patches, images, width = img.shape
     whole = patches // 16 * 16
     rest = patches - whole
-    for t in range(images):
-        panel = img[t]
-        rows = jnp.dot(panel, w_key[...], preferred_element_type=F32)
-        keys[t, 0:whole, :] = rows[0:whole].astype(BF16)
-        tail = jnp.concatenate([rows[whole:patches], jnp.zeros((16 - rest, width), F32)], axis=0)
-        keys[t, whole : whole + 16, :] = tail.astype(BF16)
-        for col in range(0, width, LANES):
-            part = jnp.dot(panel, w_value[:, col : col + LANES], preferred_element_type=F32)
-            pad = jnp.zeros((values_t.shape[2] - patches, LANES), F32)
-            values_t[t, col : col + LANES, :] = jnp.concatenate([part, pad], axis=0).T.astype(BF16)
+    body = img[0:whole].reshape(whole * images, width)
+    tail = img[whole:patches].reshape(rest * images, width)
+    tail_rows = jnp.concatenate(
+        [tail.astype(F32), jnp.zeros((16 - rest * images, width), F32)], axis=0
+    ).astype(BF16)
+    for weight, is_key in ((w_key, True), (w_value, False)):
+        for col in range(0, width, 2 * LANES):
+            double = slice(col, col + 2 * LANES)
+            product = jnp.dot(body, weight[:, double], preferred_element_type=F32)
+            last = jnp.dot(tail_rows, weight[:, double], preferred_element_type=F32)
+            for side in range(2):
+                here = slice(side * LANES, (side + 1) * LANES)
+                cols = slice(col + side * LANES, col + (side + 1) * LANES)
+                wide[side] = product[:, here]
+                for t in range(images):
+                    rows = wide[side, pl.ds(t, whole, stride=images), :]
+                    ends = [last[t + images * p : t + images * p + 1, here] for p in range(rest)]
+                    if is_key:
+                        ends.append(jnp.zeros((16 - rest, LANES), F32))
+                        keys[t, 0:whole, cols] = rows.astype(BF16)
+                        keys[t, whole : whole + 16, cols] = jnp.concatenate(ends, 0).astype(BF16)
+                    else:
+                        pad = jnp.zeros((values_t.shape[2] - patches, LANES), F32)
+                        rows = jnp.concatenate([rows, *ends, pad], axis=0)
+                        values_t[t, cols, :] = rows.T.astype(BF16)
+
+
+def spread_lanes(ref):
+    return jnp.concatenate([ref[row : row + 1, :] for row in range(ref.shape[0])], axis=1)
+
+
+def plan(cand_ids, cand_slot, requests, select, cap_local):
+    mem_size = requests.shape[0]
+    images, cands = cand_ids.shape
+    pairs = [(t, j) for t in range(images) for j in range(cands)]
+    owners = [lax.div(cand_ids[t, j], cap_local) for t, j in pairs]
+    rows = [lax.rem(cand_ids[t, j], cap_local) for t, j in pairs]
+    shape = (max(mem_size, len(pairs)), LANES)
+    sub = lax.broadcasted_iota(jnp.int32, shape, 0)
+    lane = lax.broadcasted_iota(jnp.int32, shape, 1)
+    slot_key = jnp.where(lane < SLOTS, sub * SLOTS + lane, -1)
+    table = jnp.zeros(shape, jnp.int32)
+    slot_of = jnp.zeros(shape, jnp.int32)
+    for n, (t, j) in enumerate(pairs):
+        slot = owners[n] * SLOTS
+        for before in range(n):
+            slot = slot + jnp.where(owners[before] == owners[n], 1, 0)
+        table = jnp.where(slot_key == slot, rows[n], table)
+        slot_of = jnp.where(sub == t * cands + cand_slot[t, j], slot, slot_of)
+    for shard in range(mem_size):
+        requests[shard] = table[shard : shard + 1, :]
+    word = lax.broadcasted_iota(jnp.int32, (PIECE, LANES), 0)
+    wanted_rows = jnp.concatenate(
+        [
+            jnp.broadcast_to(slot_of[n : n + 1, :], (PIECE, LANES)) * PIECE + word
+            for n in range(len(pairs))
+        ],
+        axis=0,
+    )
+    for col in range(0, select.shape[1], LANES):
+        here = lax.broadcasted_iota(jnp.int32, wanted_rows.shape, 1) + col
+        select[:, col : col + LANES] = jnp.where(wanted_rows == here, 1.0, 0.0).astype(BF16)
 
 
 def head_pair_scores(queries, keys, t, col, rows):
@@ -95,8 +147,8 @@
 def kernel(
     mem_size,
     dp_size,
-    requests,
-    targets,
+    cand_ids,
+    cand_slot,
     out_bias,
     gain1,
     shift1,
@@ -121,6 +173,8 @@
     w_out,
     w_up,
     w_down,
+    wide,
+    requests,
     wanted,
     wanted_smem,
     outgoing,
@@ -144,8 +198,7 @@
     mem = lax.axis_index("mem")
     words = cache.shape[1]
     piece_count = words // PIECE
-    patches = img.shape[1]
-    images = img.shape[0]
+    patches, images = img.shape[0:2]
 
     loads = [
         pltpu.make_async_copy(source, target, local_sem.at[index])
@@ -177,6 +230,7 @@
         pl.semaphore_signal(
             barrier, inc=1, device_id=(lax.rem(dp + step, dp_size), mem), device_id_type=MESH
         )
+    plan(cand_ids, cand_slot, requests, select, cache.shape[0])
     pl.semaphore_wait(barrier, mem_size - 1 + dp_size - 1)
 
     def ask(step, carry):
@@ -194,11 +248,6 @@
     lax.fori_loop(1, mem_size, ask, 0)
     wanted[mem] = requests[mem]
 
-    row_targets = targets[...]
-    for col in range(0, select.shape[1], LANES):
-        lane = lax.broadcasted_iota(jnp.int32, row_targets.shape, 1) + col
-        select[:, col : col + LANES] = jnp.where(row_targets == lane, 1.0, 0.0).astype(BF16)
-
     others = pl.ds(0, mem_size - 1)
     pltpu.make_async_copy(wanted.at[others], wanted.at[others], ask_recv).wait()
     to_smem = pltpu.make_async_copy(wanted, wanted_smem, smem_sem)
@@ -217,7 +266,7 @@
         incoming[piece, mem] = rows_for(mem, piece * PIECE)
 
         def serve(step, carry, piece=piece):
-            peer = lax.rem(mem + step, mem_size)
+            peer = lax.rem(mem + lax.rem(step * 13, mem_size), mem_size)
             outgoing[piece, peer] = rows_for(peer, piece * PIECE)
             pltpu.make_async_remote_copy(
                 src_ref=outgoing.at[piece, peer],
@@ -233,7 +282,7 @@
 
     for load in loads[1:4]:
         load.wait()
-    project_images(img, w_key, w_value, keys, values_t)
+    project_images(img, w_key, w_value, keys, values_t, wide)
     for load in loads[4:]:
         load.wait()
 
@@ -251,13 +300,13 @@
         attend(queries, keys, values_t, context, patches)
         attended = jnp.dot(context[...], w_out[...], preferred_element_type=F32)
         first_out = normalize(
-            attended + out_bias[...] + text_rows.astype(F32), gain1[...], shift1[...]
+            attended + spread_lanes(out_bias) + text_rows.astype(F32), spread_lanes(gain1), spread_lanes(shift1)
         ).astype(BF16)
-        hidden = jnp.dot(first_out, w_up[...], preferred_element_type=F32) + up_bias[...]
+        hidden = jnp.dot(first_out, w_up[...], preferred_element_type=F32) + spread_lanes(up_bias)
         hidden = (0.5 * hidden * (1.0 + lax.erf(hidden * 0.5**0.5))).astype(BF16)
         output = jnp.dot(hidden, w_down[...], preferred_element_type=F32)
-        output = output + down_bias[...] + first_out.astype(F32)
-        encoded = normalize(output, gain2[...], shift2[...]).astype(BF16)
+        output = output + spread_lanes(down_bias) + first_out.astype(F32)
+        encoded = normalize(output, spread_lanes(gain2), spread_lanes(shift2)).astype(BF16)
         for t in range(images):
             for group in range(dp_size):
                 start = (t * dp_size + group) * half_rows
@@ -320,7 +369,7 @@
     mem_size = lax.axis_size("mem")
     dp_size = lax.axis_size("dp")
     img_local, cand_count = cand_ids.shape
-    cap_local, word_count, width = text_cache.shape
+    word_count, width = text_cache.shape[1:]
     patches = images.shape[1]
     hidden_width = w_up.shape[1]
     pair_count = img_local * cand_count
@@ -330,47 +379,26 @@
     padded = -(-patches // 16) * 16
     padded_lanes = -(-patches // LANES) * LANES
 
-    flat_ids = cand_ids.reshape(pair_count)
-    owner_of = flat_ids // cap_local
-    local_row = flat_ids % cap_local
-    position = jnp.arange(pair_count, dtype=jnp.int32)
-    same_owner = (owner_of[:, None] == owner_of[None, :]) & (position[None, :] < position[:, None])
-    owner_rank = jnp.sum(same_owner.astype(jnp.int32), axis=1)
-    slot_index = owner_of * SLOTS + owner_rank
-    table_slots = (
-        jnp.arange(mem_size, dtype=jnp.int32)[:, None] * SLOTS
-        + jnp.arange(LANES, dtype=jnp.int32)[None, :]
-    )
-    table_slots = jnp.where(jnp.arange(LANES)[None, :] < SLOTS, table_slots, -1)
-    requests = jnp.sum(
-        jnp.where(slot_index[None, None, :] == table_slots[:, :, None], local_row, 0), axis=2
-    ).reshape(mem_size, 1, LANES)
-
-    slot_ids = jnp.arange(cand_count, dtype=jnp.int32)
-    matches = cand_slot[:, :, None] == slot_ids[None, None, :]
-    slot_of = jnp.sum(
-        jnp.where(matches, slot_index.reshape(img_local, cand_count, 1), 0), axis=1
-    ).reshape(pair_count)
-    targets = slot_of[:, None] * PIECE + jnp.arange(PIECE, dtype=jnp.int32)[None, :]
-    targets = jnp.broadcast_to(targets.reshape(piece_rows, 1), (piece_rows, LANES))
-
     vmem = pl.BlockSpec(memory_space=pltpu.VMEM)
+    smem = pl.BlockSpec(memory_space=pltpu.SMEM)
     anywhere = pl.BlockSpec(memory_space=pl.ANY)
     group_rows = piece_rows // dp_size
     result = pl.pallas_call(
         functools.partial(kernel, mem_size, dp_size),
         out_shape=jax.ShapeDtypeStruct((piece_count, dp_size, group_rows, width), BF16),
-        in_specs=[vmem] * 9 + [anywhere] * 8,
+        in_specs=[smem] * 2 + [vmem] * 7 + [anywhere] * 8,
         out_specs=anywhere,
         scratch_shapes=[
             pltpu.VMEM(text_cache.shape, BF16),
-            pltpu.VMEM(images.shape, BF16),
+            pltpu.VMEM((patches, img_local, width), BF16),
             pltpu.VMEM((width, width), BF16),
             pltpu.VMEM((width, width), BF16),
             pltpu.VMEM((width, width), BF16),
             pltpu.VMEM((width, width), BF16),
             pltpu.VMEM((width, hidden_width), BF16),
             pltpu.VMEM((hidden_width, width), BF16),
+            pltpu.VMEM((2, patches // 16 * 16 * img_local, LANES), F32),
+            pltpu.VMEM((mem_size, 1, LANES), jnp.int32),
             pltpu.VMEM((mem_size, 1, LANES), jnp.int32),
             pltpu.SMEM((mem_size, 1, LANES), jnp.int32),
             pltpu.VMEM((piece_count, mem_size, slot_rows, width), BF16),
@@ -394,17 +422,22 @@
             collective_id=0, has_side_effects=True, vmem_limit_bytes=60 * 2**20
         ),
     )(
-        requests,
-        targets,
-        out_bias.reshape(1, width),
-        norm1_gain.reshape(1, width),
-        norm1_shift.reshape(1, width),
-        up_bias.reshape(1, hidden_width),
-        down_bias.reshape(1, width),
-        norm2_gain.reshape(1, width),
-        norm2_shift.reshape(1, width),
+        cand_ids,
+        cand_slot,
+        *(
+            vector.reshape(-1, LANES)
+            for vector in (
+                out_bias,
+                norm1_gain,
+                norm1_shift,
+                up_bias,
+                down_bias,
+                norm2_gain,
+                norm2_shift,
+            )
+        ),
         text_cache,
-        images,
+        images.transpose(1, 0, 2),
         w_key,
         w_value,
         w_query,

time: 115 us -> 77.9 us (0.68)
  the two profiles are of different devices: /device:TPU:19 before, /device:TPU:1 now
where the time goes in v2:
time: 77.9 us; the launch traced here: 77.7 us
  Pallas kernels  74.7 us (96%)
  local copies, waits for them, and re-layouts  2.94 us (4%)
    pallas_call x1, Pallas kernels, on_device(): pl.pallas_call(functools.partial(kernel, mem_size, dp_size), out_shape=ja...  74.7 us
    transpose x1, local copies, waits for them, and re-layouts, on_device(): result.transpose(1, 2, 0, 3, 4).reshape(pair_count, word_count, width)  2.94 us

profile of v2, /device:TPU:1, one launch (start us, length us, event | category | flops | bytes accessed | tf_op | source)
XLA Modules:
  0.0 77.7 jit_solution(16181885663225244919)
XLA Ops:
  0.0 74.7 %shard_map.163 = bf16[5,4,64,768]{3,2,1,0:T(8,128)(2,1)} custom-call(s32[2,16]{1,0:T(2,128)} %cand_ids.1, s32[2,16]{1,0:T(2,128)} %cand_slot.1, f32[6,128]{1,0:T(8,128)} %bitcast.15, f32[6,128]{1,0:T(8,128)} %bitcast.16, f32[6,128]{1,0:T(8,128)} %bitcast.17, f32[24,128]{1,0:T(8,128)} %bitcast.14, f32[6,128]{1,0:T(8,128)} %bitcast.18, f32[6,128]{1,0:T(8,128)} %bitcast.19, ...), custom_call_target="tpu_custom_call" | custom-call | tf_op jit(solution)/shard_map/pallas_call | solution.py:386
  74.7 2.9 %copy.18 = bf16[4,8,5,8,768]{4,3,2,1,0:T(8,128)(2,1)} copy(bf16[4,8,5,8,768]{4,3,1,0,2:T(8,128)(2,1)} %bitcast.12) | data formatting | bytes 3932160 | tf_op jit(solution)/shard_map/transpose | solution.py:450

commit v3 on v2

--- a/solution.py
+++ b/solution.py
@@ -13,7 +13,8 @@
 BF16 = jnp.bfloat16
 HEADS = 12
 NORM_EPS = 1e-06
-PIECE = 8
+PIECE = 4
+PAIRED = 2
 SLOTS = 2
 LANES = 128
 NT = (((1,), (1,)), ((), ()))
@@ -25,7 +26,7 @@
     return center * lax.rsqrt(spread + NORM_EPS) * gain + shift
 
 
-def project_images(img, w_key, w_value, keys, values_t, wide):
+def project_images(img, weight, wide, store):
     patches, images, width = img.shape
     whole = patches // 16 * 16
     rest = patches - whole
@@ -34,26 +35,37 @@
     tail_rows = jnp.concatenate(
         [tail.astype(F32), jnp.zeros((16 - rest * images, width), F32)], axis=0
     ).astype(BF16)
-    for weight, is_key in ((w_key, True), (w_value, False)):
-        for col in range(0, width, 2 * LANES):
-            double = slice(col, col + 2 * LANES)
-            product = jnp.dot(body, weight[:, double], preferred_element_type=F32)
-            last = jnp.dot(tail_rows, weight[:, double], preferred_element_type=F32)
-            for side in range(2):
-                here = slice(side * LANES, (side + 1) * LANES)
-                cols = slice(col + side * LANES, col + (side + 1) * LANES)
-                wide[side] = product[:, here]
-                for t in range(images):
-                    rows = wide[side, pl.ds(t, whole, stride=images), :]
-                    ends = [last[t + images * p : t + images * p + 1, here] for p in range(rest)]
-                    if is_key:
-                        ends.append(jnp.zeros((16 - rest, LANES), F32))
-                        keys[t, 0:whole, cols] = rows.astype(BF16)
-                        keys[t, whole : whole + 16, cols] = jnp.concatenate(ends, 0).astype(BF16)
-                    else:
-                        pad = jnp.zeros((values_t.shape[2] - patches, LANES), F32)
-                        rows = jnp.concatenate([rows, *ends, pad], axis=0)
-                        values_t[t, cols, :] = rows.T.astype(BF16)
+    for col in range(0, width, 2 * LANES):
+        double = slice(col, col + 2 * LANES)
+        product = jnp.dot(body, weight[:, double], preferred_element_type=F32)
+        last = jnp.dot(tail_rows, weight[:, double], preferred_element_type=F32)
+        for side in range(2):
+            here = slice(side * LANES, (side + 1) * LANES)
+            wide[side] = product[:, here]
+            for t in range(images):
+                rows = wide[side, pl.ds(t, whole, stride=images), :]
+                ends = [last[t + images * p : t + images * p + 1, here] for p in range(rest)]
+                store(t, col + side * LANES, rows, ends)
+
+
+def project_keys(img, w_key, keys, wide):
+    def store(t, col, rows, ends):
+        cols = slice(col, col + LANES)
+        whole, rest = rows.shape[0], len(ends)
+        ends = [*ends, jnp.zeros((16 - rest, LANES), F32)]
+        keys[t, 0:whole, cols] = rows.astype(BF16)
+        keys[t, whole : whole + 16, cols] = jnp.concatenate(ends, axis=0).astype(BF16)
+
+    project_images(img, w_key, wide, store)
+
+
+def project_values(img, w_value, values_t, wide):
+    def store(t, col, rows, ends):
+        pad = jnp.zeros((values_t.shape[2] - rows.shape[0] - len(ends), LANES), F32)
+        rows = jnp.concatenate([rows, *ends, pad], axis=0)
+        values_t[t, col : col + LANES, :] = rows.T.astype(BF16)
+
+    project_images(img, w_value, wide, store)
 
 
 def spread_lanes(ref):
@@ -93,55 +105,54 @@
         select[:, col : col + LANES] = jnp.where(wanted_rows == here, 1.0, 0.0).astype(BF16)
 
 
-def head_pair_scores(queries, keys, t, col, rows):
-    both = queries[t * rows : (t + 1) * rows, col : col + LANES].astype(F32)
-    first = lax.broadcasted_iota(jnp.int32, both.shape, 1) < LANES // 2
-    stacked = jnp.concatenate([jnp.where(first, both, 0.0), jnp.where(first, 0.0, both)], axis=0)
+def head_scores(queries, keys, t, col, rows, span, head_dim):
+    these = queries[t * rows : (t + 1) * rows, col : col + span].astype(F32)
+    head = lax.broadcasted_iota(jnp.int32, these.shape, 1) // head_dim
+    stacked = jnp.concatenate(
+        [jnp.where(head == h, these, 0.0) for h in range(span // head_dim)], axis=0
+    )
     return lax.dot_general(
-        keys[t, :, col : col + LANES], stacked.astype(BF16), NT, preferred_element_type=F32
+        keys[t, :, col : col + span], stacked.astype(BF16), NT, preferred_element_type=F32
     )
 
 
 def exponentials(scores, patches, scale):
     whole = patches // 16 * 16
-    body, tail = scores[0:whole], scores[whole:]
+    tail = scores[whole:]
     row = lax.broadcasted_iota(jnp.int32, tail.shape, 0)
     tail = jnp.where(row < patches - whole, tail, -1e30)
     top = jnp.maximum(
-        jnp.max(body, axis=0, keepdims=True), jnp.max(tail, axis=0, keepdims=True)
+        jnp.max(scores[0:whole], axis=0, keepdims=True), jnp.max(tail, axis=0, keepdims=True)
     )
     factor = scale * math.log2(math.e)
-    body = jnp.exp2((body - top) * factor)
-    tail = jnp.exp2((tail - top) * factor)
-    total = jnp.sum(body, axis=0, keepdims=True) + jnp.sum(tail, axis=0, keepdims=True)
-    return jnp.concatenate([body, tail], axis=0).astype(BF16), total
+    parts, total = [], 0.0
+    for start in range(0, whole + 16, 16):
+        part = tail if start == whole else scores[start : start + 16]
+        part = jnp.exp2((part - top) * factor)
+        parts.append(part.astype(BF16))
+        total = total + part
+    return jnp.concatenate(parts, axis=0), jnp.sum(total, axis=0, keepdims=True)
 
 
 def attend(queries, keys, values_t, context, patches):
     images, padded, width = keys.shape
     rows = queries.shape[0] // images
-    half = LANES // 2
-    scale = (width // HEADS) ** (-0.5)
-    order = [(t, col) for t in range(images) for col in range(0, width, LANES)]
-    scores = head_pair_scores(queries, keys, *order[0], rows)
-    for index, (t, col) in enumerate(order):
-        following = None
-        if index + 1 < len(order):
-            following = head_pair_scores(queries, keys, *order[index + 1], rows)
-        probs, total = exponentials(scores, patches, scale)
-        mixed = jnp.dot(
-            values_t[t, col : col + LANES, 0:padded], probs, preferred_element_type=F32
+    head_dim = width // HEADS
+    span = 2 * LANES // rows * head_dim
+    scale = head_dim ** (-0.5)
+    order = [(t, col) for t in range(images) for col in range(0, width, span)]
+    scores = [head_scores(queries, keys, t, col, rows, span, head_dim) for t, col in order]
+    probs = [exponentials(one, patches, scale) for one in scores]
+    for (t, col), (one, total) in zip(order, probs):
+        mixed = jnp.dot(values_t[t, col : col + span, 0:padded], one, preferred_element_type=F32)
+        mixed = mixed * (1.0 / total)
+        own = [
+            mixed[h * head_dim : (h + 1) * head_dim, h * rows : (h + 1) * rows]
+            for h in range(span // head_dim)
+        ]
+        context[t * rows : (t + 1) * rows, col : col + span] = (
+            jnp.concatenate(own, axis=0).T.astype(BF16)
         )
-        inverse = 1.0 / total
-        mixed = jnp.concatenate(
-            [
-                mixed[0:half, 0:rows] * inverse[:, 0:rows],
-                mixed[half:LANES, rows:] * inverse[:, rows:],
-            ],
-            axis=0,
-        )
-        context[t * rows : (t + 1) * rows, col : col + LANES] = mixed.T.astype(BF16)
-        scores = following
 
 
 def kernel(
@@ -248,6 +259,10 @@
     lax.fori_loop(1, mem_size, ask, 0)
     wanted[mem] = requests[mem]
 
+    for load in loads[1:3]:
+        load.wait()
+    project_keys(img, w_key, keys, wide)
+
     others = pl.ds(0, mem_size - 1)
     pltpu.make_async_copy(wanted.at[others], wanted.at[others], ask_recv).wait()
     to_smem = pltpu.make_async_copy(wanted, wanted_smem, smem_sem)
@@ -255,34 +270,52 @@
     loads[0].wait()
     to_smem.wait()
 
-    def rows_for(peer, start):
-        parts = [
-            cache[wanted_smem[peer, 0, slot], start : start + PIECE, :].astype(F32)
+    def gather(peer, first):
+        start = first * PIECE
+        slots = [
+            cache[wanted_smem[peer, 0, slot], start : start + PAIRED * PIECE, :].astype(F32)
             for slot in range(SLOTS)
         ]
-        return jnp.concatenate(parts, axis=0).astype(BF16)
-
-    for piece in range(piece_count):
-        incoming[piece, mem] = rows_for(mem, piece * PIECE)
-
-        def serve(step, carry, piece=piece):
-            peer = lax.rem(mem + lax.rem(step * 13, mem_size), mem_size)
-            outgoing[piece, peer] = rows_for(peer, piece * PIECE)
-            pltpu.make_async_remote_copy(
-                src_ref=outgoing.at[piece, peer],
-                dst_ref=incoming.at[piece, mem],
-                send_sem=text_send.at[piece],
-                recv_sem=text_recv.at[piece],
-                device_id=(dp, peer),
-                device_id_type=MESH,
-            ).start()
+        return [
+            jnp.concatenate([rows[k * PIECE : (k + 1) * PIECE] for rows in slots], 0).astype(BF16)
+            for k in range(PAIRED)
+        ]
+
+    def send(piece, peer):
+        pltpu.make_async_remote_copy(
+            src_ref=outgoing.at[piece, peer],
+            dst_ref=incoming.at[piece, mem],
+            send_sem=text_send.at[piece],
+            recv_sem=text_recv.at[piece],
+            device_id=(dp, peer),
+            device_id_type=MESH,
+        ).start()
+
+    def partner(step):
+        return lax.rem(mem + lax.rem(step * 13, mem_size), mem_size)
+
+    for first in range(0, piece_count, PAIRED):
+        for k, rows in enumerate(gather(mem, first)):
+            incoming[first + k, mem] = rows
+
+        def serve(step, carry, first=first):
+            peer = partner(step)
+            for k, rows in enumerate(gather(peer, first)):
+                outgoing[first + k, peer] = rows
+            send(first, peer)
             return carry
 
+        def serve_next(step, carry, first=first):
+            send(first + 1, partner(step))
+            return carry
+
         lax.fori_loop(1, mem_size, serve, 0)
-
-    for load in loads[1:4]:
-        load.wait()
-    project_images(img, w_key, w_value, keys, values_t, wide)
+        lax.fori_loop(1, mem_size, serve_next, 0)
+
+        if first == 0:
+            loads[3].wait()
+            project_values(img, w_value, values_t, wide)
+
     for load in loads[4:]:
         load.wait()
 
@@ -345,6 +378,13 @@
     pltpu.make_async_copy(came, came, out_recv).wait()
     own = arrived_out.at[:, pl.ds(0, 1)]
     pltpu.make_async_copy(own, own, own_sem).wait()
+
+
+def assemble(arrived, out):
+    pieces = [arrived[piece, 0].astype(F32) for piece in range(arrived.shape[0])]
+    for pair in range(out.shape[0]):
+        rows = slice(pair * PIECE, (pair + 1) * PIECE)
+        out[pair] = jnp.concatenate([piece[rows] for piece in pieces], axis=0).astype(BF16)
 
 
 def on_device(
@@ -446,8 +486,14 @@
         w_down,
     )
     pairs = pair_count // dp_size
-    result = result.reshape(piece_count, dp_size, pairs, PIECE, width)
-    return result.transpose(1, 2, 0, 3, 4).reshape(pair_count, word_count, width)
+    return pl.pallas_call(
+        assemble,
+        grid=(dp_size,),
+        out_shape=jax.ShapeDtypeStruct((pair_count, word_count, width), BF16),
+        in_specs=[pl.BlockSpec((piece_count, 1, group_rows, width), lambda s: (0, s, 0, 0))],
+        out_specs=pl.BlockSpec((pairs, word_count, width), lambda s: (s, 0, 0)),
+        compiler_params=pltpu.CompilerParams(vmem_limit_bytes=60 * 2**20),
+    )(result)
 
 
 def solution(mesh):

time: 77.9 us -> 75.1 us (0.964)
  local copies, waits for them, and re-layouts: 2.94 us -> 0 us
    pallas_call x0 -> x1, Pallas kernels: none -> 3.93 us  [on_device(): pl.pallas_call(assemble, grid=(dp_size,), out_shape=jax.ShapeDtypeStruct(...]
    pallas_call x1, Pallas kernels: 74.7 us -> 70.8 us  [on_device(): pl.pallas_call(functools.partial(kernel, mem_size, dp_size), out_shape=ja...]
    transpose x1 -> x0, local copies, waits for them, and re-layouts: 2.94 us -> none  [on_device(): result.transpose(1, 2, 0, 3, 4).reshape(pair_count, word_count, width)]
where the time goes in v3:
time: 75.1 us; the launch traced here: 74.8 us
  Pallas kernels  74.8 us (100%)
    pallas_call x1, Pallas kernels, on_device(): pl.pallas_call(functools.partial(kernel, mem_size, dp_size), out_shape=ja...  70.8 us
    pallas_call x1, Pallas kernels, on_device(): pl.pallas_call(assemble, grid=(dp_size,), out_shape=jax.ShapeDtypeStruct(...  3.93 us

profile of v3, /device:TPU:1, one launch (start us, length us, event | category | flops | bytes accessed | tf_op | source)
XLA Modules:
  0.0 74.8 jit_solution(3081533819634199756)
XLA Ops:
  0.0 70.8 %shard_map.163.arrived = bf16[10,4,32,768]{3,2,1,0:T(8,128)(2,1)} custom-call(s32[2,16]{1,0:T(2,128)} %cand_ids.1, s32[2,16]{1,0:T(2,128)} %cand_slot.1, f32[6,128]{1,0:T(8,128)} %bitcast.10, f32[6,128]{1,0:T(8,128)} %bitcast.11, f32[6,128]{1,0:T(8,128)} %bitcast.12, f32[24,128]{1,0:T(8,128)} %bitcast.9, f32[6,128]{1,0:T(8,128)} %bitcast.13, ...), custom_call_target="tpu_custom_call" | custom-call | tf_op jit(solution)/shard_map/pallas_call | solution.py:426
  70.8 3.9 %shard_map.164 = bf16[32,40,768]{2,1,0:T(8,128)(2,1)} custom-call(bf16[10,4,32,768]{3,2,1,0:T(8,128)(2,1)} %shard_map.163.arrived), custom_call_target="tpu_custom_call" | custom-call | tf_op jit(solution)/shard_map/pallas_call | solution.py:489

commit v4 on v3

--- a/solution.py
+++ b/solution.py
@@ -194,6 +194,7 @@
     keys,
     values_t,
     context,
+    unfinished,
     finished,
     local_sem,
     smem_sem,
@@ -211,6 +212,18 @@
     piece_count = words // PIECE
     patches, images = img.shape[0:2]
 
+    barrier = pltpu.get_barrier_semaphore()
+
+    def greet(step, carry):
+        peer = lax.rem(mem + step, mem_size)
+        pl.semaphore_signal(barrier, inc=1, device_id=(dp, peer), device_id_type=MESH)
+        return carry
+
+    lax.fori_loop(1, mem_size, greet, 0)
+    for step in range(1, dp_size):
+        pl.semaphore_signal(
+            barrier, inc=1, device_id=(lax.rem(dp + step, dp_size), mem), device_id_type=MESH
+        )
     loads = [
         pltpu.make_async_copy(source, target, local_sem.at[index])
         for index, (source, target) in enumerate(
@@ -229,18 +242,6 @@
     for load in loads:
         load.start()
 
-    barrier = pltpu.get_barrier_semaphore()
-
-    def greet(step, carry):
-        peer = lax.rem(mem + step, mem_size)
-        pl.semaphore_signal(barrier, inc=1, device_id=(dp, peer), device_id_type=MESH)
-        return carry
-
-    lax.fori_loop(1, mem_size, greet, 0)
-    for step in range(1, dp_size):
-        pl.semaphore_signal(
-            barrier, inc=1, device_id=(lax.rem(dp + step, dp_size), mem), device_id_type=MESH
-        )
     plan(cand_ids, cand_slot, requests, select, cache.shape[0])
     pl.semaphore_wait(barrier, mem_size - 1 + dp_size - 1)
 
@@ -322,31 +323,19 @@
     group_rows = finished.shape[2]
     half_rows = group_rows // images
 
-    def work(piece, carry):
-        pltpu.make_async_copy(
-            incoming.at[piece, others], incoming.at[piece, others], text_recv.at[piece]
-        ).wait()
-        arrived = incoming[piece].reshape(-1, incoming.shape[3])
-        text = jnp.dot(select[...], arrived, preferred_element_type=F32)
-        text_rows = text.astype(BF16)
-        queries = jnp.dot(text_rows, w_query[...], preferred_element_type=F32).astype(BF16)
-        attend(queries, keys, values_t, context, patches)
-        attended = jnp.dot(context[...], w_out[...], preferred_element_type=F32)
-        first_out = normalize(
-            attended + spread_lanes(out_bias) + text_rows.astype(F32), spread_lanes(gain1), spread_lanes(shift1)
+    def finish(piece):
+        encoded = normalize(
+            unfinished[...], spread_lanes(gain2), spread_lanes(shift2)
         ).astype(BF16)
-        hidden = jnp.dot(first_out, w_up[...], preferred_element_type=F32) + spread_lanes(up_bias)
-        hidden = (0.5 * hidden * (1.0 + lax.erf(hidden * 0.5**0.5))).astype(BF16)
-        output = jnp.dot(hidden, w_down[...], preferred_element_type=F32)
-        output = output + spread_lanes(down_bias) + first_out.astype(F32)
-        encoded = normalize(output, spread_lanes(gain2), spread_lanes(shift2)).astype(BF16)
         for t in range(images):
             for group in range(dp_size):
                 start = (t * dp_size + group) * half_rows
                 finished[piece, group, t * half_rows : (t + 1) * half_rows, :] = encoded[
                     start : start + half_rows
                 ]
-        for step in range(1, dp_size):
+
+    def send_finished(piece):
+        for step in sorted(range(1, dp_size), key=lambda hops: -min(hops, dp_size - hops)):
             peer = lax.rem(dp + step, dp_size)
             pltpu.make_async_remote_copy(
                 src_ref=finished.at[piece, peer],
@@ -359,9 +348,39 @@
         pltpu.make_async_copy(
             finished.at[piece, dp], arrived_out.at[piece, dp], own_sem
         ).start()
+
+    def work(piece, carry):
+        pltpu.make_async_copy(
+            incoming.at[piece, others], incoming.at[piece, others], text_recv.at[piece]
+        ).wait()
+        before = lax.max(piece - 1, 0)
+        finish(before)
+        arrived = incoming[piece].reshape(-1, incoming.shape[3])
+        text = jnp.dot(select[...], arrived, preferred_element_type=F32)
+        text_rows = text.astype(BF16)
+        queries = jnp.dot(text_rows, w_query[...], preferred_element_type=F32).astype(BF16)
+
+        @pl.when(piece > 0)
+        def _():
+            send_finished(before)
+
+        attend(queries, keys, values_t, context, patches)
+        attended = jnp.dot(context[...], w_out[...], preferred_element_type=F32)
+        first_out = normalize(
+            attended + spread_lanes(out_bias) + text_rows.astype(F32),
+            spread_lanes(gain1),
+            spread_lanes(shift1),
+        ).astype(BF16)
+        hidden = jnp.dot(first_out, w_up[...], preferred_element_type=F32) + spread_lanes(up_bias)
+        hidden = (0.5 * hidden * (1.0 + lax.erf(hidden * 0.5**0.5))).astype(BF16)
+        output = jnp.dot(hidden, w_down[...], preferred_element_type=F32)
+        unfinished[...] = output + spread_lanes(down_bias) + first_out.astype(F32)
         return carry
 
+    unfinished[...] = jnp.zeros_like(unfinished)
     lax.fori_loop(0, piece_count, work, 0)
+    finish(piece_count - 1)
+    send_finished(piece_count - 1)
 
     pltpu.make_async_copy(requests.at[others], requests.at[others], ask_send).wait()
 
@@ -380,11 +399,32 @@
     pltpu.make_async_copy(own, own, own_sem).wait()
 
 
-def assemble(arrived, out):
-    pieces = [arrived[piece, 0].astype(F32) for piece in range(arrived.shape[0])]
-    for pair in range(out.shape[0]):
-        rows = slice(pair * PIECE, (pair + 1) * PIECE)
-        out[pair] = jnp.concatenate([piece[rows] for piece in pieces], axis=0).astype(BF16)
+def assemble(arrived_hbm, out_hbm, arrived, out, in_sem, out_sem):
+    sources, pieces, rows = arrived.shape[0:3]
+    pairs = rows // PIECE
+    loads = [
+        pltpu.make_async_copy(arrived_hbm.at[:, source], arrived.at[source], in_sem.at[source])
+        for source in range(sources)
+    ]
+    stores = [
+        pltpu.make_async_copy(
+            out.at[pl.ds(source * pairs, pairs)],
+            out_hbm.at[pl.ds(source * pairs, pairs)],
+            out_sem.at[source],
+        )
+        for source in range(sources)
+    ]
+    for load in loads:
+        load.start()
+    for source in range(sources):
+        loads[source].wait()
+        parts = [arrived[source, piece].astype(F32) for piece in range(pieces)]
+        for pair in range(pairs):
+            words = [part[pair * PIECE : (pair + 1) * PIECE] for part in parts]
+            out[source * pairs + pair] = jnp.concatenate(words, axis=0).astype(BF16)
+        stores[source].start()
+    for store in stores:
+        store.wait()
 
 
 def on_device(
@@ -447,6 +487,7 @@
             pltpu.VMEM((img_local, padded, width), BF16),
             pltpu.VMEM((img_local, width, padded_lanes), BF16),
             pltpu.VMEM((piece_rows, width), BF16),
+            pltpu.VMEM((piece_rows, width), F32),
             pltpu.VMEM((piece_count, dp_size, group_rows, width), BF16),
             pltpu.SemaphoreType.DMA((8,)),
             pltpu.SemaphoreType.DMA,
@@ -485,13 +526,17 @@
         w_up,
         w_down,
     )
-    pairs = pair_count // dp_size
     return pl.pallas_call(
         assemble,
-        grid=(dp_size,),
         out_shape=jax.ShapeDtypeStruct((pair_count, word_count, width), BF16),
-        in_specs=[pl.BlockSpec((piece_count, 1, group_rows, width), lambda s: (0, s, 0, 0))],
-        out_specs=pl.BlockSpec((pairs, word_count, width), lambda s: (s, 0, 0)),
+        in_specs=[anywhere],
+        out_specs=anywhere,
+        scratch_shapes=[
+            pltpu.VMEM((dp_size, piece_count, group_rows, width), BF16),
+            pltpu.VMEM((pair_count, word_count, width), BF16),
+            pltpu.SemaphoreType.DMA((dp_size,)),
+            pltpu.SemaphoreType.DMA((dp_size,)),
+        ],
         compiler_params=pltpu.CompilerParams(vmem_limit_bytes=60 * 2**20),
     )(result)
 

time: 75.1 us -> 73 us (0.972)
  Pallas kernels: 74.8 us -> 72.9 us
    pallas_call x1, Pallas kernels: 3.93 us -> 2.48 us  [on_device(): pl.pallas_call(assemble, out_shape=jax.ShapeDtypeStruct((pair_count, word...]
where the time goes in v4:
time: 73 us; the launch traced here: 72.9 us
  Pallas kernels  72.9 us (100%)
    pallas_call x1, Pallas kernels, on_device(): pl.pallas_call(functools.partial(kernel, mem_size, dp_size), out_shape=ja...  70.4 us
    pallas_call x1, Pallas kernels, on_device(): pl.pallas_call(assemble, out_shape=jax.ShapeDtypeStruct((pair_count, word...  2.48 us

profile of v4, /device:TPU:1, one launch (start us, length us, event | category | flops | bytes accessed | tf_op | source)
XLA Modules:
  0.0 72.9 jit_solution(7071597153800615078)
XLA Ops:
  0.0 70.4 %shard_map.163.arrived_hbm = bf16[10,4,32,768]{3,2,1,0:T(8,128)(2,1)} custom-call(s32[2,16]{1,0:T(2,128)} %cand_ids.1, s32[2,16]{1,0:T(2,128)} %cand_slot.1, f32[6,128]{1,0:T(8,128)} %bitcast.10, f32[6,128]{1,0:T(8,128)} %bitcast.11, f32[6,128]{1,0:T(8,128)} %bitcast.12, f32[24,128]{1,0:T(8,128)} %bitcast.9, f32[6,128]{1,0:T(8,128)} %bitcast.13, ...), custom_call_target="tpu_custom_call" | custom-call | tf_op jit(solution)/shard_map/pallas_call | solution.py:466
  70.4 2.5 %shard_map.164 = bf16[32,40,768]{2,1,0:T(8,128)(2,1)} custom-call(bf16[10,4,32,768]{3,2,1,0:T(8,128)(2,1)} %shard_map.163.arrived_hbm), custom_call_target="tpu_custom_call" | custom-call | tf_op jit(solution)/shard_map/pallas_call | solution.py:529

commit v5 on v4

--- a/solution.py
+++ b/solution.py
@@ -214,8 +214,11 @@
 
     barrier = pltpu.get_barrier_semaphore()
 
+    def far_first(step):
+        return lax.rem(step + mem_size // 2 - 2, mem_size - 1) + 1
+
     def greet(step, carry):
-        peer = lax.rem(mem + step, mem_size)
+        peer = lax.rem(mem + far_first(step), mem_size)
         pl.semaphore_signal(barrier, inc=1, device_id=(dp, peer), device_id_type=MESH)
         return carry
 
@@ -246,7 +249,7 @@
     pl.semaphore_wait(barrier, mem_size - 1 + dp_size - 1)
 
     def ask(step, carry):
-        peer = lax.rem(mem + step, mem_size)
+        peer = lax.rem(mem + far_first(step), mem_size)
         pltpu.make_async_remote_copy(
             src_ref=requests.at[peer],
             dst_ref=wanted.at[mem],

time: 73 us -> 73 us (level)
  no operation moved by 1% of the time
where the time goes in v5:
time: 73 us; the launch traced here: 72.9 us
  Pallas kernels  72.8 us (100%)
    pallas_call x1, Pallas kernels, on_device(): pl.pallas_call(functools.partial(kernel, mem_size, dp_size), out_shape=ja...  70.4 us
    pallas_call x1, Pallas kernels, on_device(): pl.pallas_call(assemble, out_shape=jax.ShapeDtypeStruct((pair_count, word...  2.48 us

profile of v5, /device:TPU:1, one launch (start us, length us, event | category | flops | bytes accessed | tf_op | source)
XLA Modules:
  0.0 72.9 jit_solution(18176685906943278388)
XLA Ops:
  0.0 70.4 %shard_map.163.arrived_hbm = bf16[10,4,32,768]{3,2,1,0:T(8,128)(2,1)} custom-call(s32[2,16]{1,0:T(2,128)} %cand_ids.1, s32[2,16]{1,0:T(2,128)} %cand_slot.1, f32[6,128]{1,0:T(8,128)} %bitcast.10, f32[6,128]{1,0:T(8,128)} %bitcast.11, f32[6,128]{1,0:T(8,128)} %bitcast.12, f32[24,128]{1,0:T(8,128)} %bitcast.9, f32[6,128]{1,0:T(8,128)} %bitcast.13, ...), custom_call_target="tpu_custom_call" | custom-call | tf_op jit(solution)/shard_map/pallas_call | solution.py:469
  70.4 2.5 %shard_map.164 = bf16[32,40,768]{2,1,0:T(8,128)(2,1)} custom-call(bf16[10,4,32,768]{3,2,1,0:T(8,128)(2,1)} %shard_map.163.arrived_hbm), custom_call_target="tpu_custom_call" | custom-call | tf_op jit(solution)/shard_map/pallas_call | solution.py:532
